TPU v7x, 32 devices: a whole 2x2x4 slice. The times are simulated.
32 devices in a mesh: gx: 4 (over z), gy: 4 (over y, x), gz: 2 (over core).
Axes of the slice: x: 2, y: 2, z: 4, core: 2. Of those that a mesh axis runs over, the one named last changes fastest.
Arguments:
- positions: float32 [3, 1536, 512], P(None, ('gx', 'gy', 'gz')), may hold values from -1 to 1
- spacing: float32 [1536, 8], P(('gx', 'gy', 'gz')), may hold values from 0.0005 to 0.02
- crossings: int32 [1536, 8], P(('gx', 'gy', 'gz')), may hold values from 0 to 31, all different within a row; in each aligned block of 48 rows (0 to 47, 48 to 95, ...) at most 24 rows name the same one
- target: float32 [3, 1536], P(None, ('gx', 'gy', 'gz')), may hold values from 0 to 1
- first_weight: bfloat16 [32, 256, 60], P(('gx', 'gy', 'gz')), may hold values from -0.75 to 0.75
- head_weight: bfloat16 [32, 4, 256], P(('gx', 'gy', 'gz')), may hold values from -0.375 to 0.375
Outputs:
- rendered: float32 [3, 1536], P(None, ('gx', 'gy', 'gz'))
- first_update: float32 [32, 256, 60], P(('gx', 'gy', 'gz'))
- head_update: float32 [32, 4, 256], P(('gx', 'gy', 'gz'))
Inputs may be any that keep to these rules, and one draw needn't show every extreme that they name: `crossings`: each ray crosses 8 different bricks, in no spatial pattern over the devices. Among the rays of one device no brick is crossed more than 24 times, a bound that some block reaches.
All inputs are finite; a program needn't handle non-finite values.
Results may differ from a plain program's by a relative error of at most 0.0029.
Values sent between devices are 32-bit elements; how exact they have to be, the bound alone decides.
A program may use at most 64 MiB of HBM per device.

v0:
```python
import functools
import math

import jax
import jax.numpy as jnp
from jax import lax
from jax.experimental import pallas as pl
from jax.experimental.pallas import tpu as pltpu
from jax.sharding import PartitionSpec as P

FREQS = 10
SAMPLES = 64
SEGS = 8
AXES = ("gx", "gy", "gz")
ENC = 6 * FREQS
ROWS = ENC + 4
HID = 256
PACK = 4
LANES = PACK * SAMPLES
GATHER_LIMIT = 64
VMEM_BYTES = 58 * 1024 * 1024
HIGHEST = lax.Precision.HIGHEST


PI_VALUE = 3.141592653589793
NORM_EPS = 1e-06
BLOCK_LIMIT = 2048


def exact_dot(a, b):
    return jnp.dot(a, b, precision=HIGHEST, preferred_element_type=jnp.float32)


def iota(shape, dim):
    return lax.broadcasted_iota(jnp.int32, shape, dim)


def logistic(x):
    return 0.5 + 0.5 * jnp.tanh(0.5 * x)


def encode_block(p0, p1, p2):
    shape = (ROWS, LANES)
    row = iota((ROWS, 1), 0)
    freq = row // 6
    wave = row % 6 // 3
    axis = row % 3
    scale = jnp.zeros((ROWS, 1), jnp.float32)
    for k in range(FREQS):
        scale = jnp.where(freq == k, 2.0**k, scale)
    point = jnp.where(
        axis == 0,
        jnp.broadcast_to(p0, shape),
        jnp.where(axis == 1, jnp.broadcast_to(p1, shape), jnp.broadcast_to(p2, shape)),
    )
    turns = point * scale
    whole = jnp.round(turns)
    rest = turns - whole
    odd = jnp.abs(whole - 2.0 * jnp.round(0.5 * whole))
    sign = 1.0 - 2.0 * odd
    is_cos = (wave == 1) & (row < ENC)
    arg = jnp.where(is_cos, 0.5 - jnp.abs(rest), rest)
    square = arg * arg
    total = jnp.full(shape, -(PI_VALUE**11) / math.factorial(11), jnp.float32)
    for power in (9, 7, 5, 3, 1):
        factor = PI_VALUE**power / math.factorial(power)
        total = total * square + (factor if power % 4 == 1 else -factor)
    return (total * arg * sign).astype(jnp.bfloat16)


def rays_kernel(
    groups,
    bricks,
    ray_rows,
    brick_of,
    weights,
    staged,
    group_row,
    group_col,
    place_col,
    target,
    rendered_out,
    grads,
    weight_t,
    encoded,
    hidden,
    slope,
    points,
    outs,
    ups,
    per_entry,
):
    entries = ray_rows * SEGS
    turns = (brick_of[groups] + 1) // 2

    place = (iota((groups, entries), 0) == group_row[...]).astype(jnp.float32)
    for c in range(4):
        points[c] = exact_dot(place, staged[c])
    outs[...] = jnp.zeros_like(outs)
    grads[...] = jnp.zeros_like(grads)

    @pl.loop(0, bricks)
    def _(b):
        weight_t[b] = weights[b].T.astype(jnp.bfloat16)

    def forward(g):
        b = brick_of[g]
        enc = encode_block(*[points[c, pl.ds(g, 1), :] for c in range(3)])
        encoded[g] = enc
        before = jnp.dot(weight_t[b], enc, preferred_element_type=jnp.float32)
        sig = logistic(before)
        act = before * sig
        slope[g] = (sig + act * (1.0 - sig)).astype(jnp.bfloat16)
        hid = act.astype(jnp.bfloat16)
        hidden[g] = hid
        head = weights[b, ROWS - 8 :, :].astype(jnp.bfloat16)
        out = jnp.dot(head, hid, preferred_element_type=jnp.float32)
        for ch in range(4):
            outs[ch, pl.ds(g, 1), :] = out[4 + ch : 5 + ch, :]

    @pl.loop(0, turns)
    def _(turn):
        forward(2 * turn)
        forward(2 * turn + 1)

    same = iota((LANES, LANES), 0) // SAMPLES == iota((LANES, LANES), 1) // SAMPLES
    upto = (same & (iota((LANES, LANES), 0) <= iota((LANES, LANES), 1))).astype(jnp.float32)
    beyond = (same & (iota((LANES, LANES), 0) > iota((LANES, LANES), 1))).astype(jnp.float32)
    steps = points[3]
    raw = outs[0]
    density = jnp.maximum(raw, 0.0) + jnp.log1p(jnp.exp(-jnp.abs(raw)))
    colour = [logistic(outs[1 + c]) for c in range(3)]
    optical = density * steps
    inclusive = exact_dot(optical, upto)
    leaving = jnp.exp(-inclusive)
    weight = jnp.exp(optical - inclusive) - leaving
    lane = iota((LANES, 128), 0)
    col = iota((LANES, 128), 1)
    sums = jnp.zeros((groups, 128), jnp.float32)
    for ch in range(4):
        pick = col == 4 * ch + lane // SAMPLES
        if ch == 3:
            pick = pick & (lane % SAMPLES == SAMPLES - 1)
        sums = sums + exact_dot(weight * colour[ch] if ch < 3 else leaving, pick.astype(jnp.float32))
    back = (iota((entries, groups), 1) == group_col[...]).astype(jnp.float32)
    found = exact_dot(back, sums)
    entry_col = iota((entries, 128), 1)
    here = entry_col % 4 == place_col[...]
    values = [
        jnp.sum(jnp.where(here & (entry_col // 4 == ch), found, 0.0), axis=1, keepdims=True)
        for ch in range(4)
    ]

    def seg(ch, s):
        return values[ch][s * ray_rows : (s + 1) * ray_rows]

    prefix = [jnp.ones((ray_rows, 1), jnp.float32)]
    for s in range(SEGS - 1):
        prefix.append(prefix[s] * seg(3, s))
    residual = []
    for c in range(3):
        shown = sum(prefix[s] * seg(c, s) for s in range(SEGS))
        rendered_out[c] = shown
        residual.append(shown - target[c])
    behind = [jnp.zeros((ray_rows, 1), jnp.float32)] * 3
    for s in range(SEGS - 1, -1, -1):
        grad_trans = prefix[s] * sum(behind[c] * residual[c] for c in range(3))
        rows = pl.ds(s * ray_rows, ray_rows)
        mine = here[s * ray_rows : (s + 1) * ray_rows]
        which = entry_col[s * ray_rows : (s + 1) * ray_rows] // 4
        block = jnp.zeros((ray_rows, 128), jnp.float32)
        for ch in range(4):
            value = prefix[s] * residual[ch] if ch < 3 else grad_trans * seg(3, s)
            block = jnp.where(mine & (which == ch), value, block)
        per_entry[rows, :] = block
        behind = [seg(c, s) + seg(3, s) * behind[c] for c in range(3)]
    spread = exact_dot(place, per_entry[...])
    wide = []
    for ch in range(4):
        to_lanes = iota((128, LANES), 0) == 4 * ch + iota((128, LANES), 1) // SAMPLES
        wide.append(exact_dot(spread, to_lanes.astype(jnp.float32)))
    shading = sum(colour[c] * wide[c] for c in range(3))
    after = exact_dot(weight * shading, beyond)
    ups[0] = (shading * leaving - after - wide[3]) * steps * logistic(raw)
    for c in range(3):
        ups[1 + c] = weight * wide[c] * colour[c] * (1.0 - colour[c])

    row8 = iota((8, LANES), 0)

    def backward(g):
        b = brick_of[g]
        up8 = jnp.zeros((8, LANES), jnp.float32)
        for ch in range(4):
            line = jnp.broadcast_to(ups[ch, pl.ds(g, 1), :], (8, LANES))
            up8 = jnp.where(row8 == 4 + ch, line, up8)
        up = jnp.concatenate([jnp.zeros((ROWS - 8, LANES), jnp.float32), up8], axis=0)
        up = up.astype(jnp.bfloat16)
        grad_hidden = jnp.dot(weight_t[b], up, preferred_element_type=jnp.float32)
        grad_before = (grad_hidden * slope[g].astype(jnp.float32)).astype(jnp.bfloat16)
        dims = (((1,), (1,)), ((), ()))
        return lax.dot_general(
            encoded[g], grad_before, dims, preferred_element_type=jnp.float32
        ) + lax.dot_general(up, hidden[g], dims, preferred_element_type=jnp.float32)

    @pl.loop(0, turns)
    def _(turn):
        first = backward(2 * turn)
        second = backward(2 * turn + 1)
        grads[brick_of[2 * turn]] += first
        grads[brick_of[2 * turn + 1]] += second


def own_rays(positions, spacing, crossings, target, gathered):
    bricks = gathered.shape[0]
    ray_rows = crossings.shape[0]
    entries = ray_rows * SEGS
    groups = -(-((entries + (PACK - 1) * bricks) // PACK) // 8) * 8
    brick_ids = crossings.T.reshape(entries)
    order_rank = jnp.arange(entries, dtype=jnp.int32)
    earlier = (brick_ids[:, None] == brick_ids[None, :]) & (
        order_rank[None, :] < order_rank[:, None]
    )
    rank = jnp.sum(earlier.astype(jnp.int32), axis=1)
    all_bricks = jnp.arange(bricks, dtype=jnp.int32)
    counts = jnp.sum((brick_ids[:, None] == all_bricks[None, :]).astype(jnp.int32), axis=0)
    needed = (counts + PACK - 1) // PACK
    ends = jnp.sum(
        jnp.where(all_bricks[None, :] <= all_bricks[:, None], needed[None, :], 0), axis=1
    )
    start = jnp.sum(
        jnp.where(all_bricks[None, :] < brick_ids[:, None], needed[None, :], 0), axis=1
    )
    group = start + rank // PACK
    place = rank % PACK
    numbers = jnp.arange(groups, dtype=jnp.int32)
    brick_of = jnp.minimum(
        jnp.sum((ends[None, :] <= numbers[:, None]).astype(jnp.int32), axis=1), bricks - 1
    )
    brick_of = jnp.concatenate([brick_of, jnp.sum(needed)[None]])
    points = positions.reshape(3, ray_rows, SEGS, 1, SAMPLES).transpose(0, 2, 1, 3, 4)
    steps = jnp.broadcast_to(spacing.T[None, :, :, None, None], (1, SEGS, ray_rows, 1, SAMPLES))
    values = jnp.concatenate([points, steps], axis=0).reshape(4, entries, 1, SAMPLES)
    chosen = place[None, :, None, None] == jnp.arange(PACK, dtype=jnp.int32)[None, None, :, None]
    staged = jnp.where(chosen, values, 0.0).reshape(4, entries, LANES)
    vmem = pl.BlockSpec(memory_space=pltpu.VMEM)
    samples = groups * LANES
    rendered, grads = pl.pallas_call(
        functools.partial(rays_kernel, groups, bricks, ray_rows),
        out_shape=(
            jax.ShapeDtypeStruct((3, ray_rows, 1), jnp.float32),
            jax.ShapeDtypeStruct((bricks, ROWS, HID), jnp.float32),
        ),
        in_specs=[pl.BlockSpec(memory_space=pltpu.SMEM)] + [vmem] * 6,
        out_specs=(vmem, vmem),
        scratch_shapes=[
            pltpu.VMEM((bricks, HID, ROWS), jnp.bfloat16),
            pltpu.VMEM((groups, ROWS, LANES), jnp.bfloat16),
            pltpu.VMEM((groups, HID, LANES), jnp.bfloat16),
            pltpu.VMEM((groups, HID, LANES), jnp.bfloat16),
            pltpu.VMEM((4, groups, LANES), jnp.float32),
            pltpu.VMEM((4, groups, LANES), jnp.float32),
            pltpu.VMEM((4, groups, LANES), jnp.float32),
            pltpu.VMEM((entries, 128), jnp.float32),
        ],
        compiler_params=pltpu.CompilerParams(vmem_limit_bytes=VMEM_BYTES),
        cost_estimate=pl.CostEstimate(
            flops=samples * HID * ROWS * 10,
            transcendentals=samples * HID,
            bytes_accessed=2 * bricks * ROWS * HID * 4,
        ),
        name="own_rays",
    )(
        brick_of,
        gathered,
        staged,
        group[None, :],
        group[:, None],
        place[:, None],
        target[:, :, None],
    )
    return rendered[:, :, 0], grads


def partners(sizes):
    here = tuple(lax.axis_index(name) for name in AXES)

    def shifted(axis, step):
        place = list(here)
        place[axis] = lax.rem(here[axis] + step, sizes[axis])
        return tuple(place)

    others = [shifted(axis, step) for axis in range(3) for step in range(1, sizes[axis])]
    return here, shifted, others


def greet(others):
    barrier = pltpu.get_barrier_semaphore()
    for other in others:
        pl.semaphore_signal(barrier, inc=1, device_id=other, device_id_type=pl.DeviceIdType.MESH)
    pl.semaphore_wait(barrier, len(others))


def transfer(source, landing, send_sem, recv_sem, device):
    return pltpu.make_async_remote_copy(
        src_ref=source,
        dst_ref=landing,
        send_sem=send_sem,
        recv_sem=recv_sem,
        device_id=device,
        device_id_type=pl.DeviceIdType.MESH,
    )


def gather_kernel(sizes, own, out, sends, recvs):
    nx, ny, nz = sizes
    (x, y, z), shifted, others = partners(sizes)
    greet(others)
    out[x, y, z] = own[...]
    started = []

    def block(dx, dy, dz):
        return out.at[
            lax.rem(x - dx + nx, nx), lax.rem(y - dy + ny, ny), lax.rem(z - dz + nz, nz)
        ]

    def send(source, axis, step, came):
        where = (came[0] * ny + came[1]) * nz + came[2]
        copy = transfer(source, source, sends.at[where], recvs.at[where], shifted(axis, step))
        copy.start()
        started.append(copy)

    def arrive(came):
        where = (came[0] * ny + came[1]) * nz + came[2]
        landed = block(*came)
        transfer(landed, landed, sends.at[where], recvs.at[where], others[0]).wait_recv()

    for dx in range(1, nx):
        send(block(0, 0, 0), 0, dx, (dx, 0, 0))
    for dx in range(nx):
        if dx > 0:
            arrive((dx, 0, 0))
        for dy in range(1, ny):
            send(block(dx, 0, 0), 1, dy, (dx, dy, 0))
        for dz in range(1, nz):
            send(block(dx, 0, 0), 2, dz, (dx, 0, dz))
    for dx in range(nx):
        for dy in range(1, ny):
            arrive((dx, dy, 0))
            for dz in range(1, nz):
                send(block(dx, dy, 0), 2, dz, (dx, dy, dz))
    for dx in range(nx):
        for dy in range(ny):
            for dz in range(1, nz):
                arrive((dx, dy, dz))
    for copy in started:
        copy.wait_send()


def gather_weights(packed, sizes):
    count = sizes[0] * sizes[1] * sizes[2]
    vmem = pl.BlockSpec(memory_space=pltpu.VMEM)
    gathered = pl.pallas_call(
        functools.partial(gather_kernel, sizes),
        out_shape=jax.ShapeDtypeStruct(sizes + packed.shape, jnp.float32),
        in_specs=[vmem],
        out_specs=vmem,
        scratch_shapes=[pltpu.SemaphoreType.DMA((count,)), pltpu.SemaphoreType.DMA((count,))],
        compiler_params=pltpu.CompilerParams(
            collective_id=0, has_side_effects=True, vmem_limit_bytes=VMEM_BYTES
        ),
        name="gather_weights",
    )(packed)
    return gathered.reshape((count,) + packed.shape)


def update_kernel(
    sizes, grads, out, from_z, sum_z, from_y, sum_y, from_x, parts, sends, recvs, small_s, small_r
):
    nx, ny, nz = sizes
    (x, y, z), shifted, others = partners(sizes)
    greet(others)
    started = []

    def place(step, axis):
        return lax.rem((x, y, z)[axis] + step, sizes[axis])

    def number(step):
        return (step[0] * ny + step[1]) * nz + step[2]

    def send(source, landing, where, axis, step):
        copy = transfer(source, landing, sends.at[where], recvs.at[where], shifted(axis, step))
        copy.start()
        started.append(copy)

    def arrive(landing, where):
        transfer(landing, landing, sends.at[where], recvs.at[where], others[0]).wait_recv()

    order_x = list(range(1, nx)) + [0]
    order_y = list(range(1, ny)) + [0]
    for dx in order_x:
        for dy in order_y:
            for dz in range(1, nz):
                send(
                    grads.at[place(dx, 0), place(dy, 1), place(dz, 2)],
                    from_z.at[dx, dy, dz - 1],
                    number((dx, dy, dz)),
                    2,
                    dz,
                )
    for dx in order_x:
        for dy in order_y:
            total = grads[place(dx, 0), place(dy, 1), z]
            for dz in range(1, nz):
                arrive(from_z.at[dx, dy, dz - 1], number((dx, dy, dz)))
                total = total + from_z[dx, dy, dz - 1]
            sum_z[dx, dy] = total
            if dy > 0:
                send(sum_z.at[dx, dy], from_y.at[dx, dy - 1], number((dx, dy, 0)), 1, dy)
    for dx in order_x:
        total = sum_z[dx, 0]
        for dy in range(1, ny):
            arrive(from_y.at[dx, dy - 1], number((dx, dy, 0)))
            total = total + from_y[dx, dy - 1]
        sum_y[dx] = total
        if dx > 0:
            send(sum_y.at[dx], from_x.at[dx - 1], number((dx, 0, 0)), 0, dx)
    for dx in range(1, nx):
        arrive(from_x.at[dx - 1], number((dx, 0, 0)))
        total = total + from_x[dx - 1]
    square = total * total
    part = jnp.zeros((8, 128), jnp.float32)
    for i in range(0, square.shape[0], 8):
        for j in range(0, square.shape[1], 128):
            part = part + square[i : i + 8, j : j + 128]
    slot = 0
    for axis in range(3):
        parts[slot] = part
        copies = []
        for step in range(1, sizes[axis]):
            copy = transfer(
                parts.at[slot],
                parts.at[slot + step],
                small_s.at[slot + step],
                small_r.at[slot + step],
                shifted(axis, step),
            )
            copy.start()
            copies.append(copy)
        for step in range(1, sizes[axis]):
            copies[step - 1].wait_recv()
            part = part + parts[slot + step]
        started.extend(copies)
        slot += sizes[axis]
    overall = jnp.sum(part, keepdims=True)
    count_all = nx * ny * nz * total.size
    out[...] = total * lax.rsqrt(overall / count_all + NORM_EPS)
    for copy in started:
        copy.wait_send()


def sum_and_scale(grads, sizes):
    nx, ny, nz = sizes
    count = nx * ny * nz
    tile = grads.shape[1:]
    vmem = pl.BlockSpec(memory_space=pltpu.VMEM)
    small = nx + ny + nz
    return pl.pallas_call(
        functools.partial(update_kernel, sizes),
        out_shape=jax.ShapeDtypeStruct(tile, jnp.float32),
        in_specs=[vmem],
        out_specs=vmem,
        scratch_shapes=[
            pltpu.VMEM((nx, ny, max(nz - 1, 1)) + tile, jnp.float32),
            pltpu.VMEM((nx, ny) + tile, jnp.float32),
            pltpu.VMEM((nx, max(ny - 1, 1)) + tile, jnp.float32),
            pltpu.VMEM((nx,) + tile, jnp.float32),
            pltpu.VMEM((max(nx - 1, 1),) + tile, jnp.float32),
            pltpu.VMEM((small, 8, 128), jnp.float32),
            pltpu.SemaphoreType.DMA((count,)),
            pltpu.SemaphoreType.DMA((count,)),
            pltpu.SemaphoreType.DMA((small,)),
            pltpu.SemaphoreType.DMA((small,)),
        ],
        compiler_params=pltpu.CompilerParams(
            collective_id=1, has_side_effects=True, vmem_limit_bytes=VMEM_BYTES
        ),
        name="sum_and_scale",
    )(grads.reshape(sizes + tile))


def by_gather(positions, spacing, crossings, target, first_weight, head_weight):
    sizes = tuple(lax.axis_size(name) for name in AXES)
    packed = jnp.concatenate(
        [first_weight[0].astype(jnp.float32).T, head_weight[0].astype(jnp.float32)], axis=0
    )
    gathered = gather_weights(packed, sizes)
    rendered, grads = own_rays(positions, spacing, crossings, target, gathered)
    scaled = sum_and_scale(grads, sizes)
    return (rendered, scaled[:ENC].T[None], scaled[ENC:][None])


def encode(points):
    scales = 2.0 ** jnp.arange(FREQS, dtype=jnp.float32) * PI_VALUE
    angles = scales[:, None, None] * points[None]
    wave_table = jnp.stack([jnp.sin(angles), jnp.cos(angles)], axis=1)
    return wave_table.reshape(6 * FREQS, points.shape[1]).astype(jnp.bfloat16)


def network(first_local, head_local, points):
    encoded = encode(points)
    before = jnp.dot(first_local, encoded, preferred_element_type=jnp.float32)
    hidden = jax.nn.silu(before).astype(jnp.bfloat16)
    output = jnp.dot(head_local, hidden, preferred_element_type=jnp.float32)
    return (encoded, before, hidden, output)


def activate(output):
    return (jax.nn.softplus(output[0]), jax.nn.sigmoid(output[1:]))


def segment_forward(density, colour, step_len):
    optical = density * step_len[:, None]
    inclusive = jnp.cumsum(optical, axis=1)
    leaving = jnp.exp(-inclusive)
    weight = jnp.exp(optical - inclusive) - leaving
    seg_colour = jnp.sum(weight[None] * colour, axis=2)
    return (seg_colour, leaving[:, -1], weight, leaving)


def segment_backward(colour, weight, leaving, step_len, grad_colour, grad_trans):
    shading = jnp.sum(colour * grad_colour[:, :, None], axis=0)
    weighted = weight * shading
    after = jnp.sum(weighted, axis=1, keepdims=True) - jnp.cumsum(weighted, axis=1)
    grad_depth = shading * leaving - after - (grad_trans * leaving[:, -1])[:, None]
    grad_density = grad_depth * step_len[:, None]
    grad_sample = weight[None] * grad_colour[:, :, None]
    return (grad_density, grad_sample)


def ray_level(seg_colour, seg_trans, target):
    seg_total = seg_trans.shape[1]
    through = jnp.cumprod(seg_trans, axis=1)
    prefix = jnp.concatenate([jnp.ones_like(seg_trans[:, :1]), through[:, :-1]], axis=1)
    rendered = jnp.sum(prefix[None] * seg_colour, axis=2)
    residual = rendered - target
    grad_colour = prefix[None] * residual[:, :, None]
    behind_list = [jnp.zeros_like(rendered)]
    for offset in range(seg_total - 1, 0, -1):
        behind_list.append(seg_colour[:, :, offset] + seg_trans[:, offset][None] * behind_list[-1])
    behind = jnp.stack(behind_list[::-1], axis=2)
    grad_trans = prefix * jnp.sum(behind * residual[:, :, None], axis=0)
    return (rendered, grad_colour, grad_trans)


def output_grad(output, grad_density, grad_sample):
    colour = jax.nn.sigmoid(output[1:])
    first_row = grad_density * jax.nn.sigmoid(output[0])
    others = grad_sample * colour * (1.0 - colour)
    return jnp.concatenate([first_row[None], others], axis=0).astype(jnp.bfloat16)


def network_grad(head_local, encoded, before, hidden, upstream):
    grad_head = lax.dot_general(
        upstream, hidden, (((1,), (1,)), ((), ())), preferred_element_type=jnp.float32
    )
    grad_hidden = lax.dot_general(
        head_local, upstream, (((0,), (0,)), ((), ())), preferred_element_type=jnp.float32
    )
    logistic = jax.nn.sigmoid(before)
    grad_before = (grad_hidden * logistic * (1.0 + before * (1.0 - logistic))).astype(jnp.bfloat16)
    grad_first = lax.dot_general(
        grad_before, encoded, (((1,), (1,)), ((), ())), preferred_element_type=jnp.float32
    )
    return (grad_first, grad_head)


def by_exchange(positions, spacing, crossings, target, first_weight, head_weight):
    across = lax.axis_size(("gx", "gy"))
    along_count = lax.axis_size("gz")
    devices = across * along_count
    ray_rows = crossings.shape[0]
    entries = ray_rows * SEGS
    capacity = 2 * entries // devices
    total_slots = devices * capacity
    sample_total = total_slots * SAMPLES
    block_size = math.gcd(sample_total, BLOCK_LIMIT)
    block_count = sample_total // block_size
    block_segs = block_size // SAMPLES
    first_local = first_weight[0]
    head_local = head_weight[0]
    brick_ids = crossings.reshape(entries)
    order_rank = jnp.arange(entries, dtype=jnp.int32)
    earlier = (brick_ids[:, None] == brick_ids[None, :]) & (
        order_rank[None, :] < order_rank[:, None]
    )
    column = brick_ids * capacity + jnp.sum(earlier.astype(jnp.int32), axis=1)
    own_points = positions.reshape(3, entries, SAMPLES)
    own_steps = spacing.reshape(entries)
    send_points = jnp.zeros((3, total_slots, SAMPLES), jnp.float32).at[:, column, :].set(own_points)
    send_steps = jnp.zeros((1, total_slots), jnp.float32).at[0, column].set(own_steps)
    got_points, got_steps = (
        lax.all_to_all(
            lax.all_to_all(
                send_points.reshape(3, across, along_count, capacity * SAMPLES),
                ("gx", "gy"),
                split_axis=1,
                concat_axis=1,
                tiled=True,
            ),
            "gz",
            split_axis=2,
            concat_axis=2,
            tiled=True,
        ),
        lax.all_to_all(
            lax.all_to_all(
                send_steps.reshape(1, across, along_count, capacity),
                ("gx", "gy"),
                split_axis=1,
                concat_axis=1,
                tiled=True,
            ),
            "gz",
            split_axis=2,
            concat_axis=2,
            tiled=True,
        ),
    )
    point_blocks = got_points.reshape(3, block_count, block_size).transpose(1, 0, 2)
    step_blocks = got_steps.reshape(block_count, block_segs)

    def forward_turn(unused, inputs):
        block_points, block_steps = inputs
        encoded, before, hidden, output = network(first_local, head_local, block_points)
        density, colour = activate(output)
        result = jnp.concatenate([density[None], colour], axis=0)
        return (unused, result)

    unused, results = lax.scan(
        forward_turn, jnp.zeros((), jnp.float32), (point_blocks, step_blocks)
    )
    values = results.transpose(1, 0, 2).reshape(4, across, along_count, capacity * SAMPLES)
    returned = lax.all_to_all(
        lax.all_to_all(values, ("gx", "gy"), split_axis=1, concat_axis=1, tiled=True),
        "gz",
        split_axis=2,
        concat_axis=2,
        tiled=True,
    )
    owned = returned.reshape(4, total_slots, SAMPLES)[:, column, :]
    seg_colour, seg_trans, weight, leaving = segment_forward(owned[0], owned[1:], own_steps)
    rendered, grad_colour, grad_trans = ray_level(
        seg_colour.reshape(3, ray_rows, SEGS), seg_trans.reshape(ray_rows, SEGS), target
    )
    grad_density, grad_sample = segment_backward(
        owned[1:],
        weight,
        leaving,
        own_steps,
        grad_colour.reshape(3, entries),
        grad_trans.reshape(entries),
    )
    stacked = jnp.concatenate([grad_density[None], grad_sample], axis=0)
    send_grads = jnp.zeros((4, total_slots, SAMPLES), jnp.float32).at[:, column, :].set(stacked)
    got_grads = lax.all_to_all(
        lax.all_to_all(
            send_grads.reshape(4, across, along_count, capacity * SAMPLES),
            ("gx", "gy"),
            split_axis=1,
            concat_axis=1,
            tiled=True,
        ),
        "gz",
        split_axis=2,
        concat_axis=2,
        tiled=True,
    )
    grad_blocks = got_grads.reshape(4, block_count, block_size).transpose(1, 0, 2)

    def backward_turn(totals, inputs):
        block_points, block_steps, block_upstream = inputs
        encoded, before, hidden, output = network(first_local, head_local, block_points)
        grad_density = block_upstream[0]
        grad_sample = block_upstream[1:]
        upstream = output_grad(output, grad_density, grad_sample)
        grad_first, grad_head = network_grad(head_local, encoded, before, hidden, upstream)
        return ((totals[0] + grad_first, totals[1] + grad_head), None)

    start_totals = (
        jnp.zeros(first_local.shape, jnp.float32),
        jnp.zeros(head_local.shape, jnp.float32),
    )
    totals, unused_out = lax.scan(
        backward_turn, start_totals, (point_blocks, step_blocks, grad_blocks)
    )
    grad_first, grad_head = totals
    square_sum = jnp.sum(grad_first * grad_first) + jnp.sum(grad_head * grad_head)
    overall = lax.psum(square_sum, ("gx", "gy", "gz"))
    count_all = devices * (grad_first.size + grad_head.size)
    scale = lax.rsqrt(overall / count_all + NORM_EPS)
    return (rendered, (grad_first * scale)[None], (grad_head * scale)[None])


def solution(mesh):
    in_specs = (
        P(None, ("gx", "gy", "gz"), None),
        P(("gx", "gy", "gz"), None),
        P(("gx", "gy", "gz"), None),
        P(None, ("gx", "gy", "gz")),
        P(("gx", "gy", "gz"), None, None),
        P(("gx", "gy", "gz"), None, None),
    )
    out_specs = (
        P(None, ("gx", "gy", "gz")),
        P(("gx", "gy", "gz"), None, None),
        P(("gx", "gy", "gz"), None, None),
    )
    body = by_gather if mesh.size <= GATHER_LIMIT else by_exchange
    return jax.shard_map(
        body, mesh=mesh, in_specs=in_specs, out_specs=out_specs, check_vma=False
    )
```

profile of v0, /device:TPU:1, one launch (start us, length us, event | category | flops | bytes accessed | tf_op | source)
XLA Modules:
  0.0 139.8 jit_solution(15774497898915910975)
XLA Ops:
  0.6 0.8 eq.50
  1.4 0.1 convert_reduce_fusion.1
  1.5 0.7 fusion.13
  2.2 0.1 select_reduce_fusion.1
  2.3 0.1 convert_reduce_fusion.2
  2.4 1.2 pad_add_fusion.brick_of
  3.6 0.1 select_reduce_fusion
  3.7 0.2 convert_reduce_fusion
  3.9 0.6 fusion.12.group_row
  4.5 1.4 %maximum_convert_fusion.own = f32[64,256]{1,0:T(8,128)} fusion(bf16[4,256]{1,0:T(4,128)(2,1)} %bitcast.31, bf16[60,256]{1,0:T(8,128)(2,1)} %bitcast.28), kind=kLoop, calls=%fused_computation.26 | loop fusion | flops 65536 | bytes 98304 | tf_op jit(solution)/shard_map/concatenate | solution.py:493
  5.9 1.4 %copy.29.target = f32[3,48,1]{2,1,0:T(8,128)} copy(f32[3,48,1]{1,0,2:T(4,128)} %bitcast.32) | data formatting | bytes 1152 | tf_op jit(solution)/shard_map/broadcast_in_dim | solution.py:279
  7.4 0.2 copy.21
  7.6 0.7 broadcast_in_dim.91
  8.3 1.0 add_select_fusion
  9.3 1.1 reshape.223
  10.4 0.3 copy.22
  10.7 0.1 pad_maximum_fusion
  10.8 0.3 broadcast_in_dim.92
  11.1 0.1 broadcast_in_dim.93
  11.3 0.5 copy.23
  11.8 1.3 broadcast_select_fusion.staged
  13.1 22.7 %gather_weights.1 = f32[4,4,2,64,256]{4,3,2,1,0:T(8,128)} custom-call(f32[64,256]{1,0:T(8,128)} %maximum_convert_fusion.own), custom_call_target="tpu_custom_call" | custom-call | tf_op jit(solution)/shard_map/gather_weights/pallas_call | solution.py:362
  35.9 69.4 %own_rays.1 = (f32[3,48,1]{2,1,0:T(8,128)}, f32[32,64,256]{2,1,0:T(8,128)}) custom-call(s32[121]{0:T(128)} %pad_add_fusion.brick_of, f32[32,64,256]{2,1,0:T(8,128)} %bitcast.26, f32[4,384,256]{2,1,0:T(8,128)} %broadcast_select_fusion.staged, s32[1,384]{1,0:T(1,128)} %fusion.12.group_row, s32[384,1]{1,0:T(8,128)} %get-tuple-element.19.group_col, ...), custom_call_target="tpu_custom_call" | custom-call | flops 5033164800 | bytes 4194304 | tf_op jit(solution)/shard_map/own_rays/pallas_call | solution.py:247
  105.3 1.6 %reduce = f32[3,48]{1,0:T(4,128)} reduce(f32[3,48,1]{2,1,0:T(8,128)} %get-tuple-element.5, f32[]{:T(128)} %constant.55), dimensions={2}, to_apply=%get-tuple-element.5.reduce_sub_computation | reduce | bytes 1156 | tf_op jit(solution)/shard_map/own_rays/pallas_call | solution.py:247
  106.9 30.1 %sum_and_scale.1 = f32[64,256]{1,0:T(8,128)} custom-call(f32[4,4,2,64,256]{4,3,2,1,0:T(8,128)} %bitcast.25), custom_call_target="tpu_custom_call" | custom-call | tf_op jit(solution)/shard_map/sum_and_scale/pallas_call | solution.py:467
  136.9 1.3 slice_bitcast_fusion.1
  138.2 0.8 slice_bitcast_fusion
  139.1 0.7 copy.30
  (4 shorter events, 0.1 us)
where the time goes:
time: 140 us
  Pallas kernels  122 us (87%)
  other arithmetic  8.5 us (6%)
  local copies, waits for them, and re-layouts  8.32 us (6%)
    pallas_call x1, Pallas kernels, own_rays(): pl.pallas_call(functools.partial(rays_kernel, groups, bricks, ray_rows),...  69.4 us
    pallas_call x1, Pallas kernels, sum_and_scale(): pl.pallas_call(functools.partial(update_kernel, sizes), out_shape=jax.Sha...  30.1 us
    pallas_call x1, Pallas kernels, gather_weights(): pl.pallas_call(functools.partial(gather_kernel, sizes), out_shape=jax.Sha...  22.7 us

commit v1 on v0

--- a/solution.py
+++ b/solution.py
@@ -68,13 +68,88 @@
     return (total * arg * sign).astype(jnp.bfloat16)
 
 
+def to_column(row):
+    n = row.shape[1]
+    return jnp.sum(jnp.where(iota((n, n), 0) == iota((n, n), 1), row, 0.0), axis=1, keepdims=True)
+
+
+def to_row(column):
+    n = column.shape[0]
+    return jnp.sum(
+        jnp.where(iota((n, n), 0) == iota((n, n), 1), column, 0.0), axis=0, keepdims=True
+    )
+
+
+def number_groups(bricks, crossings, group_row, group_col, place_col, brick_of):
+    ids_col = jnp.concatenate(
+        [to_column(crossings[s : s + 1, :].astype(jnp.float32)) for s in range(SEGS)], axis=0
+    )
+    entries = ids_col.shape[0]
+    ids_row = to_row(ids_col)
+    square = (entries, entries)
+    same = ids_col == ids_row
+    rank_col = jnp.sum(
+        jnp.where(same & (iota(square, 1) < iota(square, 0)), 1.0, 0.0), axis=1, keepdims=True
+    )
+    rank_row = jnp.sum(
+        jnp.where(same & (iota(square, 0) < iota(square, 1)), 1.0, 0.0), axis=0, keepdims=True
+    )
+    wide = 128
+    of_brick = ids_col == iota((entries, wide), 1).astype(jnp.float32)
+    counts = jnp.sum(jnp.where(of_brick, 1.0, 0.0), axis=0, keepdims=True)
+    needed_row = jnp.floor((counts + (PACK - 1)) * (1.0 / PACK))
+    needed_col = to_column(needed_row)
+    pair = (wide, wide)
+    start_row = jnp.sum(
+        jnp.where(iota(pair, 0) < iota(pair, 1), needed_col, 0.0), axis=0, keepdims=True
+    )
+    start_col = to_column(start_row)
+    first_col = jnp.sum(jnp.where(of_brick, start_row, 0.0), axis=1, keepdims=True)
+    of_brick_t = ids_row == iota((wide, entries), 0).astype(jnp.float32)
+    first_row = jnp.sum(jnp.where(of_brick_t, start_col, 0.0), axis=0, keepdims=True)
+    full_col = jnp.floor(rank_col * (1.0 / PACK))
+    full_row = jnp.floor(rank_row * (1.0 / PACK))
+    group_col[...] = (first_col + full_col).astype(jnp.int32)
+    group_row[...] = (first_row + full_row).astype(jnp.int32)
+    place_col[...] = (rank_col - PACK * full_col).astype(jnp.int32)
+    shape = (wide, brick_of.shape[1])
+    number = iota(shape, 1).astype(jnp.float32)
+    passed = (start_col + needed_col <= number) & (iota(shape, 0) < bricks)
+    found = jnp.sum(jnp.where(passed, 1.0, 0.0), axis=0, keepdims=True)
+    total = jnp.sum(needed_row, axis=1, keepdims=True)
+    last = iota(brick_of.shape, 1) == brick_of.shape[1] - 1
+    brick_of[...] = jnp.where(last, total, jnp.minimum(found, bricks - 1.0)).astype(jnp.int32)
+
+
+def place_points(groups, positions, spacing, group_row, place_col, points, steps):
+    ray_rows = positions.shape[1]
+    entries = ray_rows * SEGS
+    place = (iota((groups, entries), 0) == group_row[...]).astype(jnp.float32)
+    chosen = place_col[...] == iota((entries, LANES), 1) // SAMPLES
+    low = iota((ray_rows, 2 * SAMPLES), 1) < SAMPLES
+    for c in range(3):
+        parts = []
+        for pair in range(SEGS // 2):
+            both = positions[c, :, 2 * SAMPLES * pair : 2 * SAMPLES * (pair + 1)]
+            turned = pltpu.roll(both, SAMPLES, 1)
+            for half in (jnp.where(low, both, turned), jnp.where(low, turned, both)):
+                parts.append(jnp.concatenate([half] * (LANES // (2 * SAMPLES)), axis=1))
+        values = jnp.where(chosen, jnp.concatenate(parts, axis=0), 0.0)
+        points[c] = exact_dot(place, values)
+    lengths = jnp.concatenate(
+        [to_column(spacing[s : s + 1, :]) for s in range(SEGS)], axis=0
+    )
+    steps[...] = exact_dot(place, jnp.where(chosen, lengths, 0.0))
+
+
 def rays_kernel(
     groups,
     bricks,
     ray_rows,
-    brick_of,
+    brick_list,
     weights,
-    staged,
+    encoded,
+    steps_in,
     group_row,
     group_col,
     place_col,
@@ -82,32 +157,29 @@
     rendered_out,
     grads,
     weight_t,
-    encoded,
     hidden,
     slope,
-    points,
     outs,
     ups,
     per_entry,
 ):
     entries = ray_rows * SEGS
-    turns = (brick_of[groups] + 1) // 2
-
+    together = 4
+    turns = (brick_list[0, brick_list.shape[1] - 1] + together - 1) // together
     place = (iota((groups, entries), 0) == group_row[...]).astype(jnp.float32)
-    for c in range(4):
-        points[c] = exact_dot(place, staged[c])
     outs[...] = jnp.zeros_like(outs)
     grads[...] = jnp.zeros_like(grads)
 
-    @pl.loop(0, bricks)
-    def _(b):
-        weight_t[b] = weights[b].T.astype(jnp.bfloat16)
+    few = math.gcd(bricks, 4)
+
+    @pl.loop(0, bricks // few)
+    def _(turn):
+        for i in range(few):
+            weight_t[few * turn + i] = weights[few * turn + i].T.astype(jnp.bfloat16)
 
     def forward(g):
-        b = brick_of[g]
-        enc = encode_block(*[points[c, pl.ds(g, 1), :] for c in range(3)])
-        encoded[g] = enc
-        before = jnp.dot(weight_t[b], enc, preferred_element_type=jnp.float32)
+        b = brick_list[0, g]
+        before = jnp.dot(weight_t[b], encoded[g], preferred_element_type=jnp.float32)
         sig = logistic(before)
         act = before * sig
         slope[g] = (sig + act * (1.0 - sig)).astype(jnp.bfloat16)
@@ -120,13 +192,13 @@
 
     @pl.loop(0, turns)
     def _(turn):
-        forward(2 * turn)
-        forward(2 * turn + 1)
+        for i in range(together):
+            forward(together * turn + i)
 
     same = iota((LANES, LANES), 0) // SAMPLES == iota((LANES, LANES), 1) // SAMPLES
     upto = (same & (iota((LANES, LANES), 0) <= iota((LANES, LANES), 1))).astype(jnp.float32)
     beyond = (same & (iota((LANES, LANES), 0) > iota((LANES, LANES), 1))).astype(jnp.float32)
-    steps = points[3]
+    steps = steps_in[...]
     raw = outs[0]
     density = jnp.maximum(raw, 0.0) + jnp.log1p(jnp.exp(-jnp.abs(raw)))
     colour = [logistic(outs[1 + c]) for c in range(3)]
@@ -160,8 +232,8 @@
     residual = []
     for c in range(3):
         shown = sum(prefix[s] * seg(c, s) for s in range(SEGS))
-        rendered_out[c] = shown
-        residual.append(shown - target[c])
+        rendered_out[c : c + 1, :] = to_row(shown)
+        residual.append(shown - to_column(target[c : c + 1, :]))
     behind = [jnp.zeros((ray_rows, 1), jnp.float32)] * 3
     for s in range(SEGS - 1, -1, -1):
         grad_trans = prefix[s] * sum(behind[c] * residual[c] for c in range(3))
@@ -188,7 +260,7 @@
     row8 = iota((8, LANES), 0)
 
     def backward(g):
-        b = brick_of[g]
+        b = brick_list[0, g]
         up8 = jnp.zeros((8, LANES), jnp.float32)
         for ch in range(4):
             line = jnp.broadcast_to(ups[ch, pl.ds(g, 1), :], (8, LANES))
@@ -204,60 +276,30 @@
 
     @pl.loop(0, turns)
     def _(turn):
-        first = backward(2 * turn)
-        second = backward(2 * turn + 1)
-        grads[brick_of[2 * turn]] += first
-        grads[brick_of[2 * turn + 1]] += second
-
-
-def own_rays(positions, spacing, crossings, target, gathered):
+        terms = [backward(together * turn + i) for i in range(together)]
+        for i in range(together):
+            grads[brick_list[0, together * turn + i]] += terms[i]
+
+
+def own_rays(gathered, encoded, steps, group_row, group_col, place_col, brick_of, target):
     bricks = gathered.shape[0]
-    ray_rows = crossings.shape[0]
+    ray_rows = target.shape[1]
     entries = ray_rows * SEGS
-    groups = -(-((entries + (PACK - 1) * bricks) // PACK) // 8) * 8
-    brick_ids = crossings.T.reshape(entries)
-    order_rank = jnp.arange(entries, dtype=jnp.int32)
-    earlier = (brick_ids[:, None] == brick_ids[None, :]) & (
-        order_rank[None, :] < order_rank[:, None]
-    )
-    rank = jnp.sum(earlier.astype(jnp.int32), axis=1)
-    all_bricks = jnp.arange(bricks, dtype=jnp.int32)
-    counts = jnp.sum((brick_ids[:, None] == all_bricks[None, :]).astype(jnp.int32), axis=0)
-    needed = (counts + PACK - 1) // PACK
-    ends = jnp.sum(
-        jnp.where(all_bricks[None, :] <= all_bricks[:, None], needed[None, :], 0), axis=1
-    )
-    start = jnp.sum(
-        jnp.where(all_bricks[None, :] < brick_ids[:, None], needed[None, :], 0), axis=1
-    )
-    group = start + rank // PACK
-    place = rank % PACK
-    numbers = jnp.arange(groups, dtype=jnp.int32)
-    brick_of = jnp.minimum(
-        jnp.sum((ends[None, :] <= numbers[:, None]).astype(jnp.int32), axis=1), bricks - 1
-    )
-    brick_of = jnp.concatenate([brick_of, jnp.sum(needed)[None]])
-    points = positions.reshape(3, ray_rows, SEGS, 1, SAMPLES).transpose(0, 2, 1, 3, 4)
-    steps = jnp.broadcast_to(spacing.T[None, :, :, None, None], (1, SEGS, ray_rows, 1, SAMPLES))
-    values = jnp.concatenate([points, steps], axis=0).reshape(4, entries, 1, SAMPLES)
-    chosen = place[None, :, None, None] == jnp.arange(PACK, dtype=jnp.int32)[None, None, :, None]
-    staged = jnp.where(chosen, values, 0.0).reshape(4, entries, LANES)
+    groups = encoded.shape[0]
     vmem = pl.BlockSpec(memory_space=pltpu.VMEM)
     samples = groups * LANES
-    rendered, grads = pl.pallas_call(
+    return pl.pallas_call(
         functools.partial(rays_kernel, groups, bricks, ray_rows),
         out_shape=(
-            jax.ShapeDtypeStruct((3, ray_rows, 1), jnp.float32),
+            jax.ShapeDtypeStruct((3, ray_rows), jnp.float32),
             jax.ShapeDtypeStruct((bricks, ROWS, HID), jnp.float32),
         ),
-        in_specs=[pl.BlockSpec(memory_space=pltpu.SMEM)] + [vmem] * 6,
+        in_specs=[pl.BlockSpec(memory_space=pltpu.SMEM)] + [vmem] * 7,
         out_specs=(vmem, vmem),
         scratch_shapes=[
             pltpu.VMEM((bricks, HID, ROWS), jnp.bfloat16),
-            pltpu.VMEM((groups, ROWS, LANES), jnp.bfloat16),
             pltpu.VMEM((groups, HID, LANES), jnp.bfloat16),
             pltpu.VMEM((groups, HID, LANES), jnp.bfloat16),
-            pltpu.VMEM((4, groups, LANES), jnp.float32),
             pltpu.VMEM((4, groups, LANES), jnp.float32),
             pltpu.VMEM((4, groups, LANES), jnp.float32),
             pltpu.VMEM((entries, 128), jnp.float32),
@@ -269,16 +311,7 @@
             bytes_accessed=2 * bricks * ROWS * HID * 4,
         ),
         name="own_rays",
-    )(
-        brick_of,
-        gathered,
-        staged,
-        group[None, :],
-        group[:, None],
-        place[:, None],
-        target[:, :, None],
-    )
-    return rendered[:, :, 0], grads
+    )(brick_of, gathered, encoded, steps, group_row, group_col, place_col, target)
 
 
 def partners(sizes):
@@ -311,8 +344,32 @@
     )
 
 
-def gather_kernel(sizes, own, out, sends, recvs):
+def gather_kernel(
+    sizes,
+    groups,
+    own,
+    positions,
+    spacing,
+    crossings,
+    out,
+    encoded,
+    steps,
+    group_row,
+    group_col,
+    place_col,
+    brick_of,
+    points,
+    sends,
+    recvs,
+):
     nx, ny, nz = sizes
+
+    def encode_groups(first, end):
+        @pl.loop(first, end)
+        def _(turn):
+            for g in (2 * turn, 2 * turn + 1):
+                encoded[g] = encode_block(*[points[c, pl.ds(g, 1), :] for c in range(3)])
+
     (x, y, z), shifted, others = partners(sizes)
     greet(others)
     out[x, y, z] = own[...]
@@ -336,6 +393,7 @@
 
     for dx in range(1, nx):
         send(block(0, 0, 0), 0, dx, (dx, 0, 0))
+    number_groups(nx * ny * nz, crossings, group_row, group_col, place_col, brick_of)
     for dx in range(nx):
         if dx > 0:
             arrive((dx, 0, 0))
@@ -343,7 +401,10 @@
             send(block(dx, 0, 0), 1, dy, (dx, dy, 0))
         for dz in range(1, nz):
             send(block(dx, 0, 0), 2, dz, (dx, 0, dz))
+    place_points(groups, positions, spacing, group_row, place_col, points, steps)
+    turns = groups // 2
     for dx in range(nx):
+        encode_groups(turns * dx // nx, turns * (dx + 1) // nx)
         for dy in range(1, ny):
             arrive((dx, dy, 0))
             for dz in range(1, nz):
@@ -356,25 +417,41 @@
         copy.wait_send()
 
 
-def gather_weights(packed, sizes):
+def gather_weights(packed, positions, spacing, crossings, sizes):
     count = sizes[0] * sizes[1] * sizes[2]
+    ray_rows = crossings.shape[0]
+    entries = ray_rows * SEGS
+    groups = -(-((entries + (PACK - 1) * count) // PACK) // 8) * 8
+    listed = -(-(groups + 1) // 128) * 128
     vmem = pl.BlockSpec(memory_space=pltpu.VMEM)
-    gathered = pl.pallas_call(
-        functools.partial(gather_kernel, sizes),
-        out_shape=jax.ShapeDtypeStruct(sizes + packed.shape, jnp.float32),
-        in_specs=[vmem],
-        out_specs=vmem,
-        scratch_shapes=[pltpu.SemaphoreType.DMA((count,)), pltpu.SemaphoreType.DMA((count,))],
+    gathered, *rest = pl.pallas_call(
+        functools.partial(gather_kernel, sizes, groups),
+        out_shape=(
+            jax.ShapeDtypeStruct(sizes + packed.shape, jnp.float32),
+            jax.ShapeDtypeStruct((groups, ROWS, LANES), jnp.bfloat16),
+            jax.ShapeDtypeStruct((groups, LANES), jnp.float32),
+            jax.ShapeDtypeStruct((1, entries), jnp.int32),
+            jax.ShapeDtypeStruct((entries, 1), jnp.int32),
+            jax.ShapeDtypeStruct((entries, 1), jnp.int32),
+            jax.ShapeDtypeStruct((1, listed), jnp.int32),
+        ),
+        in_specs=[vmem] * 4,
+        out_specs=[vmem] * 7,
+        scratch_shapes=[
+            pltpu.VMEM((3, groups, LANES), jnp.float32),
+            pltpu.SemaphoreType.DMA((count,)),
+            pltpu.SemaphoreType.DMA((count,)),
+        ],
         compiler_params=pltpu.CompilerParams(
             collective_id=0, has_side_effects=True, vmem_limit_bytes=VMEM_BYTES
         ),
         name="gather_weights",
-    )(packed)
-    return gathered.reshape((count,) + packed.shape)
+    )(packed, positions, spacing.T, crossings.T)
+    return gathered.reshape((count,) + packed.shape), rest
 
 
 def update_kernel(
-    sizes, grads, out, from_z, sum_z, from_y, sum_y, from_x, parts, sends, recvs, small_s, small_r
+    sizes, grads, out_first, out_head, from_z, sum_z, from_y, sum_y, from_x, parts, sends, recvs, small_s, small_r
 ):
     nx, ny, nz = sizes
     (x, y, z), shifted, others = partners(sizes)
@@ -453,7 +530,9 @@
         slot += sizes[axis]
     overall = jnp.sum(part, keepdims=True)
     count_all = nx * ny * nz * total.size
-    out[...] = total * lax.rsqrt(overall / count_all + NORM_EPS)
+    scaled = total * lax.rsqrt(overall / count_all + NORM_EPS)
+    out_first[...] = scaled[:ENC]
+    out_head[...] = scaled[ENC:]
     for copy in started:
         copy.wait_send()
 
@@ -466,9 +545,12 @@
     small = nx + ny + nz
     return pl.pallas_call(
         functools.partial(update_kernel, sizes),
-        out_shape=jax.ShapeDtypeStruct(tile, jnp.float32),
+        out_shape=(
+            jax.ShapeDtypeStruct((ENC, tile[1]), jnp.float32),
+            jax.ShapeDtypeStruct((tile[0] - ENC, tile[1]), jnp.float32),
+        ),
         in_specs=[vmem],
-        out_specs=vmem,
+        out_specs=(vmem, vmem),
         scratch_shapes=[
             pltpu.VMEM((nx, ny, max(nz - 1, 1)) + tile, jnp.float32),
             pltpu.VMEM((nx, ny) + tile, jnp.float32),
@@ -493,10 +575,10 @@
     packed = jnp.concatenate(
         [first_weight[0].astype(jnp.float32).T, head_weight[0].astype(jnp.float32)], axis=0
     )
-    gathered = gather_weights(packed, sizes)
-    rendered, grads = own_rays(positions, spacing, crossings, target, gathered)
-    scaled = sum_and_scale(grads, sizes)
-    return (rendered, scaled[:ENC].T[None], scaled[ENC:][None])
+    gathered, rest = gather_weights(packed, positions, spacing, crossings, sizes)
+    rendered, grads = own_rays(gathered, *rest, target)
+    first, head = sum_and_scale(grads, sizes)
+    return (rendered, first.T[None], head[None])
 
 
 def encode(points):

time: 140 us -> 113 us (0.81)
  Pallas kernels: 122 us -> 108 us
  other arithmetic: 8.5 us -> 1.4 us
  local copies, waits for them, and re-layouts: 8.32 us -> 2.8 us
    pallas_call x1, Pallas kernels: 69.4 us -> 51.2 us  [own_rays(): pl.pallas_call(functools.partial(rays_kernel, groups, bricks, ray_rows),...]
    broadcast_in_dim x9 -> x0, local copies, waits for them, and re-layouts: 5.43 us -> none  [the longest x2 2.14 us: by_gather(): return (rendered, scaled[:ENC].T[None], scaled[ENC:][None])]
    pallas_call x2, Pallas kernels: 52.8 us -> 56.9 us  [the longest x1 29.5 us: sum_and_scale(): pl.pallas_call(functools.partial(update_kernel, sizes), out_shape=(jax.Sh...]
    select_n x3 -> x0, other arithmetic: 2.35 us -> none  [the longest x1 1.35 us: own_rays(): staged = jnp.where(chosen, values, 0.0).reshape(4, entries, LANES)]
    unnamed x1 -> x2, local copies, waits for them, and re-layouts: 0.69 us -> 2.8 us
    pallas_call x1 -> x0, other arithmetic: 1.56 us -> none  [own_rays(): pl.pallas_call(functools.partial(rays_kernel, groups, bricks, ray_rows),...]
    reshape x2 -> x0, local copies, waits for them, and re-layouts: 1.43 us -> none  [own_rays(): positions.reshape(3, ray_rows, SEGS, 1, SAMPLES).transpose(0, 2, 1, 3, 4)]
where the time goes in v1:
time: 113 us
  Pallas kernels  108 us (96%)
  local copies, waits for them, and re-layouts  2.8 us (2%)
  other arithmetic  1.4 us (1%)
    pallas_call x1, Pallas kernels, own_rays(): pl.pallas_call(functools.partial(rays_kernel, groups, bricks, ray_rows),...  51.2 us
    pallas_call x1, Pallas kernels, sum_and_scale(): pl.pallas_call(functools.partial(update_kernel, sizes), out_shape=(jax.Sh...  29.5 us
    pallas_call x1, Pallas kernels, gather_weights(): pl.pallas_call(functools.partial(gather_kernel, sizes, groups), out_shape...  27.4 us
    unnamed x2, local copies, waits for them, and re-layouts  2.8 us

profile of v1, /device:TPU:1, one launch (start us, length us, event | category | flops | bytes accessed | tf_op | source)
XLA Modules:
  0.0 113.0 jit_solution(2248902633225749367)
XLA Ops:
  0.6 1.4 %maximum_convert_fusion.own = f32[64,256]{1,0:T(8,128)} fusion(bf16[4,256]{1,0:T(4,128)(2,1)} %bitcast.18, bf16[60,256]{1,0:T(8,128)(2,1)} %bitcast.14), kind=kLoop, calls=%fused_computation | loop fusion | flops 65536 | bytes 98304 | tf_op jit(solution)/shard_map/concatenate | solution.py:575
  2.0 27.4 %gather_weights.1 = (f32[4,4,2,64,256]{4,3,2,1,0:T(8,128)}, bf16[120,64,256]{2,1,0:T(8,128)(2,1)}, f32[120,256]{1,0:T(8,128)}, s32[1,384]{1,0:T(1,128)}, s32[384...) custom-call(f32[64,256]{1,0:T(8,128)} %maximum_convert_fusion.own, f32[3,48,512]{2,1,0:T(8,128)} %positions.1, ...), custom_call_target="tpu_custom_call" | custom-call | tf_op jit(solution)/shard_map/gather_weights/pallas_call | solution.py:427
  29.4 51.2 %own_rays.1 = (f32[3,48]{1,0:T(4,128)}, f32[32,64,256]{2,1,0:T(8,128)}) custom-call(s32[1,128]{1,0:T(1,128)} %get-tuple-element.14.brick_list, f32[32,64,256]{2,1,0:T(8,128)} %bitcast.19, bf16[120,64,256]{2,1,0:T(8,128)(2,1)} %get-tuple-element.16.encoded, f32[120,256]{1,0:T(8,128)} %get-tuple-element.17.steps_in, s32[1,384]{1,0:T(1,128)} %get-tuple-element.18.group_row, ...), custom_call_target="tpu_custom_call" | custom-call | flops 5033164800 | bytes 4194304 | tf_op jit(solution)/shard_map/own_rays/pallas_call | solution.py:291
  80.7 29.5 %sum_and_scale.1 = (f32[60,256]{1,0:T(8,128)}, f32[4,256]{1,0:T(4,128)}) custom-call(f32[4,4,2,64,256]{4,3,2,1,0:T(8,128)} %bitcast.12), custom_call_target="tpu_custom_call" | custom-call | tf_op jit(solution)/shard_map/sum_and_scale/pallas_call | solution.py:546
  110.2 1.5 %copy.9 = f32[1,256,60]{1,0,2:T(1,128)} copy(f32[1,256,60]{1,2,0:T(8,128)} %bitcast.13) | data formatting | bytes 122880
  111.7 1.3 %copy.11 = f32[1,4,256]{2,1,0:T(4,128)} copy(f32[1,4,256]{2,1,0:T(4,128)} %bitcast.17) | data formatting | bytes 8192

commit v2 on v1

--- a/solution.py
+++ b/solution.py
@@ -43,29 +43,26 @@
     shape = (ROWS, LANES)
     row = iota((ROWS, 1), 0)
     freq = row // 6
-    wave = row % 6 // 3
     axis = row % 3
     scale = jnp.zeros((ROWS, 1), jnp.float32)
     for k in range(FREQS):
-        scale = jnp.where(freq == k, 2.0**k, scale)
+        scale = jnp.where(freq == k, 2.0 ** (k - 1), scale)
+    is_cos = (row % 6 // 3 == 1) & (row < ENC)
+    shift = jnp.where(is_cos, 0.0, 0.25)
     point = jnp.where(
         axis == 0,
         jnp.broadcast_to(p0, shape),
         jnp.where(axis == 1, jnp.broadcast_to(p1, shape), jnp.broadcast_to(p2, shape)),
     )
-    turns = point * scale
-    whole = jnp.round(turns)
-    rest = turns - whole
-    odd = jnp.abs(whole - 2.0 * jnp.round(0.5 * whole))
-    sign = 1.0 - 2.0 * odd
-    is_cos = (wave == 1) & (row < ENC)
-    arg = jnp.where(is_cos, 0.5 - jnp.abs(rest), rest)
+    turns = point * scale - shift
+    arg = 0.25 - jnp.abs(turns - jnp.round(turns))
     square = arg * arg
-    total = jnp.full(shape, -(PI_VALUE**11) / math.factorial(11), jnp.float32)
+    circle = 2.0 * PI_VALUE
+    total = jnp.full(shape, -(circle**11) / math.factorial(11), jnp.float32)
     for power in (9, 7, 5, 3, 1):
-        factor = PI_VALUE**power / math.factorial(power)
+        factor = circle**power / math.factorial(power)
         total = total * square + (factor if power % 4 == 1 else -factor)
-    return (total * arg * sign).astype(jnp.bfloat16)
+    return (total * arg).astype(jnp.bfloat16)
 
 
 def to_column(row):
@@ -157,6 +154,7 @@
     rendered_out,
     grads,
     weight_t,
+    grads_t,
     hidden,
     slope,
     outs,
@@ -168,21 +166,21 @@
     turns = (brick_list[0, brick_list.shape[1] - 1] + together - 1) // together
     place = (iota((groups, entries), 0) == group_row[...]).astype(jnp.float32)
     outs[...] = jnp.zeros_like(outs)
-    grads[...] = jnp.zeros_like(grads)
+    grads_t[...] = jnp.zeros_like(grads_t)
 
     few = math.gcd(bricks, 4)
 
     @pl.loop(0, bricks // few)
     def _(turn):
         for i in range(few):
-            weight_t[few * turn + i] = weights[few * turn + i].T.astype(jnp.bfloat16)
+            weight_t[few * turn + i] = (0.5 * weights[few * turn + i].T).astype(jnp.bfloat16)
 
     def forward(g):
         b = brick_list[0, g]
-        before = jnp.dot(weight_t[b], encoded[g], preferred_element_type=jnp.float32)
-        sig = logistic(before)
-        act = before * sig
-        slope[g] = (sig + act * (1.0 - sig)).astype(jnp.bfloat16)
+        half = jnp.dot(weight_t[b], encoded[g], preferred_element_type=jnp.float32)
+        bent = jnp.tanh(half)
+        act = half + half * bent
+        slope[g] = ((1.0 + act) + bent * (1.0 - act)).astype(jnp.bfloat16)
         hid = act.astype(jnp.bfloat16)
         hidden[g] = hid
         head = weights[b, ROWS - 8 :, :].astype(jnp.bfloat16)
@@ -271,14 +269,19 @@
         grad_before = (grad_hidden * slope[g].astype(jnp.float32)).astype(jnp.bfloat16)
         dims = (((1,), (1,)), ((), ()))
         return lax.dot_general(
-            encoded[g], grad_before, dims, preferred_element_type=jnp.float32
-        ) + lax.dot_general(up, hidden[g], dims, preferred_element_type=jnp.float32)
+            grad_before, encoded[g], dims, preferred_element_type=jnp.float32
+        ) + lax.dot_general(hidden[g], up, dims, preferred_element_type=jnp.float32)
 
     @pl.loop(0, turns)
     def _(turn):
         terms = [backward(together * turn + i) for i in range(together)]
         for i in range(together):
-            grads[brick_list[0, together * turn + i]] += terms[i]
+            grads_t[brick_list[0, together * turn + i]] += terms[i]
+
+    @pl.loop(0, bricks // few)
+    def _(turn):
+        for i in range(few):
+            grads[few * turn + i] = grads_t[few * turn + i].T
 
 
 def own_rays(gathered, encoded, steps, group_row, group_col, place_col, brick_of, target):
@@ -298,6 +301,7 @@
         out_specs=(vmem, vmem),
         scratch_shapes=[
             pltpu.VMEM((bricks, HID, ROWS), jnp.bfloat16),
+            pltpu.VMEM((bricks, HID, ROWS), jnp.float32),
             pltpu.VMEM((groups, HID, LANES), jnp.bfloat16),
             pltpu.VMEM((groups, HID, LANES), jnp.bfloat16),
             pltpu.VMEM((4, groups, LANES), jnp.float32),
@@ -347,7 +351,8 @@
 def gather_kernel(
     sizes,
     groups,
-    own,
+    own_first,
+    own_head,
     positions,
     spacing,
     crossings,
@@ -372,7 +377,8 @@
 
     (x, y, z), shifted, others = partners(sizes)
     greet(others)
-    out[x, y, z] = own[...]
+    out[x, y, z, :ENC, :] = own_first[...].astype(jnp.float32)
+    out[x, y, z, ENC:, :] = own_head[...].astype(jnp.float32)
     started = []
 
     def block(dx, dy, dz):
@@ -417,7 +423,7 @@
         copy.wait_send()
 
 
-def gather_weights(packed, positions, spacing, crossings, sizes):
+def gather_weights(first, head, positions, spacing, crossings, sizes):
     count = sizes[0] * sizes[1] * sizes[2]
     ray_rows = crossings.shape[0]
     entries = ray_rows * SEGS
@@ -427,7 +433,7 @@
     gathered, *rest = pl.pallas_call(
         functools.partial(gather_kernel, sizes, groups),
         out_shape=(
-            jax.ShapeDtypeStruct(sizes + packed.shape, jnp.float32),
+            jax.ShapeDtypeStruct(sizes + (ROWS, HID), jnp.float32),
             jax.ShapeDtypeStruct((groups, ROWS, LANES), jnp.bfloat16),
             jax.ShapeDtypeStruct((groups, LANES), jnp.float32),
             jax.ShapeDtypeStruct((1, entries), jnp.int32),
@@ -435,7 +441,7 @@
             jax.ShapeDtypeStruct((entries, 1), jnp.int32),
             jax.ShapeDtypeStruct((1, listed), jnp.int32),
         ),
-        in_specs=[vmem] * 4,
+        in_specs=[vmem] * 5,
         out_specs=[vmem] * 7,
         scratch_shapes=[
             pltpu.VMEM((3, groups, LANES), jnp.float32),
@@ -446,8 +452,8 @@
             collective_id=0, has_side_effects=True, vmem_limit_bytes=VMEM_BYTES
         ),
         name="gather_weights",
-    )(packed, positions, spacing.T, crossings.T)
-    return gathered.reshape((count,) + packed.shape), rest
+    )(first, head, positions, spacing.T, crossings.T)
+    return gathered.reshape((count, ROWS, HID)), rest
 
 
 def update_kernel(
@@ -572,10 +578,9 @@
 
 def by_gather(positions, spacing, crossings, target, first_weight, head_weight):
     sizes = tuple(lax.axis_size(name) for name in AXES)
-    packed = jnp.concatenate(
-        [first_weight[0].astype(jnp.float32).T, head_weight[0].astype(jnp.float32)], axis=0
-    )
-    gathered, rest = gather_weights(packed, positions, spacing, crossings, sizes)
+    gathered, rest = gather_weights(
+        first_weight[0].T, head_weight[0], positions, spacing, crossings, sizes
+    )
     rendered, grads = own_rays(gathered, *rest, target)
     first, head = sum_and_scale(grads, sizes)
     return (rendered, first.T[None], head[None])

time: 113 us -> 115 us (1.018)
  Pallas kernels: 108 us -> 111 us
  other arithmetic: 1.4 us -> 0 us
    pallas_call x1, Pallas kernels: 51.2 us -> 54.7 us  [own_rays(): pl.pallas_call(functools.partial(rays_kernel, groups, bricks, ray_rows),...]
    pallas_call x1, Pallas kernels: 27.4 us -> 25.4 us  [gather_weights(): pl.pallas_call(functools.partial(gather_kernel, sizes, groups), out_shape...]
    pallas_call x1, Pallas kernels: 29.5 us -> 30.9 us  [sum_and_scale(): pl.pallas_call(functools.partial(update_kernel, sizes), out_shape=(jax.Sh...]
    concatenate x1 -> x0, other arithmetic: 1.4 us -> none  [by_gather(): jnp.concatenate([first_weight[0].astype(jnp.float32).T, head_weight[0].as...]
where the time goes in v2:
time: 115 us
  Pallas kernels  111 us (97%)
  local copies, waits for them, and re-layouts  2.8 us (2%)
    pallas_call x1, Pallas kernels, own_rays(): pl.pallas_call(functools.partial(rays_kernel, groups, bricks, ray_rows),...  54.7 us
    pallas_call x1, Pallas kernels, sum_and_scale(): pl.pallas_call(functools.partial(update_kernel, sizes), out_shape=(jax.Sh...  30.9 us
    pallas_call x1, Pallas kernels, gather_weights(): pl.pallas_call(functools.partial(gather_kernel, sizes, groups), out_shape...  25.4 us
    unnamed x2, local copies, waits for them, and re-layouts  2.8 us

profile of v2, /device:TPU:1, one launch (start us, length us, event | category | flops | bytes accessed | tf_op | source)
XLA Modules:
  0.0 114.5 jit_solution(9941633705819111838)
XLA Ops:
  0.6 25.4 %gather_weights.1 = (f32[4,4,2,64,256]{4,3,2,1,0:T(8,128)}, bf16[120,64,256]{2,1,0:T(8,128)(2,1)}, f32[120,256]{1,0:T(8,128)}, s32[1,384]{1,0:T(1,128)}, s32[384...) custom-call(bf16[60,256]{1,0:T(8,128)(2,1)} %bitcast.14, bf16[4,256]{1,0:T(4,128)(2,1)} %bitcast.18, ...), custom_call_target="tpu_custom_call" | custom-call | tf_op jit(solution)/shard_map/gather_weights/pallas_call | solution.py:433
  26.1 54.7 %own_rays.1 = (f32[3,48]{1,0:T(4,128)}, f32[32,64,256]{2,1,0:T(8,128)}) custom-call(s32[1,128]{1,0:T(1,128)} %get-tuple-element.14.brick_list, f32[32,64,256]{2,1,0:T(8,128)} %bitcast.19, bf16[120,64,256]{2,1,0:T(8,128)(2,1)} %get-tuple-element.16.encoded, f32[120,256]{1,0:T(8,128)} %get-tuple-element.17.steps_in, s32[1,384]{1,0:T(1,128)} %get-tuple-element.18.group_row, ...), custom_call_target="tpu_custom_call" | custom-call | flops 5033164800 | bytes 4194304 | tf_op jit(solution)/shard_map/own_rays/pallas_call | solution.py:294
  80.8 30.9 %sum_and_scale.1 = (f32[60,256]{1,0:T(8,128)}, f32[4,256]{1,0:T(4,128)}) custom-call(f32[4,4,2,64,256]{4,3,2,1,0:T(8,128)} %bitcast.12), custom_call_target="tpu_custom_call" | custom-call | tf_op jit(solution)/shard_map/sum_and_scale/pallas_call | solution.py:552
  111.7 1.5 %copy.9 = f32[1,256,60]{1,0,2:T(1,128)} copy(f32[1,256,60]{1,2,0:T(8,128)} %bitcast.13) | data formatting | bytes 122880
  113.2 1.3 %copy.11 = f32[1,4,256]{2,1,0:T(4,128)} copy(f32[1,4,256]{2,1,0:T(4,128)} %bitcast.17) | data formatting | bytes 8192

commit v3 on v2

--- a/solution.py
+++ b/solution.py
@@ -19,7 +19,6 @@
 LANES = PACK * SAMPLES
 GATHER_LIMIT = 64
 VMEM_BYTES = 58 * 1024 * 1024
-HIGHEST = lax.Precision.HIGHEST
 
 
 PI_VALUE = 3.141592653589793
@@ -27,8 +26,26 @@
 BLOCK_LIMIT = 2048
 
 
-def exact_dot(a, b):
-    return jnp.dot(a, b, precision=HIGHEST, preferred_element_type=jnp.float32)
+def in_parts(x):
+    parts = []
+    for _ in range(3):
+        parts.append(x.astype(jnp.bfloat16))
+        x = x - parts[-1].astype(jnp.float32)
+    return parts
+
+
+def mask_times(mask, x):
+    mask = mask.astype(jnp.bfloat16)
+    return sum(
+        jnp.dot(mask, part, preferred_element_type=jnp.float32) for part in in_parts(x)[::-1]
+    )
+
+
+def times_mask(x, mask):
+    mask = mask.astype(jnp.bfloat16)
+    return sum(
+        jnp.dot(part, mask, preferred_element_type=jnp.float32) for part in in_parts(x)[::-1]
+    )
 
 
 def iota(shape, dim):
@@ -132,11 +149,11 @@
             for half in (jnp.where(low, both, turned), jnp.where(low, turned, both)):
                 parts.append(jnp.concatenate([half] * (LANES // (2 * SAMPLES)), axis=1))
         values = jnp.where(chosen, jnp.concatenate(parts, axis=0), 0.0)
-        points[c] = exact_dot(place, values)
+        points[c] = mask_times(place, values)
     lengths = jnp.concatenate(
         [to_column(spacing[s : s + 1, :]) for s in range(SEGS)], axis=0
     )
-    steps[...] = exact_dot(place, jnp.where(chosen, lengths, 0.0))
+    steps[...] = mask_times(place, jnp.where(chosen, lengths, 0.0))
 
 
 def rays_kernel(
@@ -145,7 +162,7 @@
     ray_rows,
     brick_list,
     weights,
-    encoded,
+    encoded_in,
     steps_in,
     group_row,
     group_col,
@@ -154,19 +171,22 @@
     rendered_out,
     grads,
     weight_t,
-    grads_t,
     hidden,
     slope,
     outs,
     ups,
     per_entry,
+    encoded,
+    arrived,
 ):
+    fetch = pltpu.make_async_copy(encoded_in, encoded, arrived)
+    fetch.start()
     entries = ray_rows * SEGS
-    together = 4
+    together = 8
     turns = (brick_list[0, brick_list.shape[1] - 1] + together - 1) // together
     place = (iota((groups, entries), 0) == group_row[...]).astype(jnp.float32)
     outs[...] = jnp.zeros_like(outs)
-    grads_t[...] = jnp.zeros_like(grads_t)
+    grads[...] = jnp.zeros_like(grads)
 
     few = math.gcd(bricks, 4)
 
@@ -174,6 +194,8 @@
     def _(turn):
         for i in range(few):
             weight_t[few * turn + i] = (0.5 * weights[few * turn + i].T).astype(jnp.bfloat16)
+
+    fetch.wait()
 
     def forward(g):
         b = brick_list[0, g]
@@ -201,7 +223,7 @@
     density = jnp.maximum(raw, 0.0) + jnp.log1p(jnp.exp(-jnp.abs(raw)))
     colour = [logistic(outs[1 + c]) for c in range(3)]
     optical = density * steps
-    inclusive = exact_dot(optical, upto)
+    inclusive = times_mask(optical, upto)
     leaving = jnp.exp(-inclusive)
     weight = jnp.exp(optical - inclusive) - leaving
     lane = iota((LANES, 128), 0)
@@ -211,9 +233,9 @@
         pick = col == 4 * ch + lane // SAMPLES
         if ch == 3:
             pick = pick & (lane % SAMPLES == SAMPLES - 1)
-        sums = sums + exact_dot(weight * colour[ch] if ch < 3 else leaving, pick.astype(jnp.float32))
+        sums = sums + times_mask(weight * colour[ch] if ch < 3 else leaving, pick.astype(jnp.float32))
     back = (iota((entries, groups), 1) == group_col[...]).astype(jnp.float32)
-    found = exact_dot(back, sums)
+    found = mask_times(back, sums)
     entry_col = iota((entries, 128), 1)
     here = entry_col % 4 == place_col[...]
     values = [
@@ -244,13 +266,13 @@
             block = jnp.where(mine & (which == ch), value, block)
         per_entry[rows, :] = block
         behind = [seg(c, s) + seg(3, s) * behind[c] for c in range(3)]
-    spread = exact_dot(place, per_entry[...])
+    spread = mask_times(place, per_entry[...])
     wide = []
     for ch in range(4):
         to_lanes = iota((128, LANES), 0) == 4 * ch + iota((128, LANES), 1) // SAMPLES
-        wide.append(exact_dot(spread, to_lanes.astype(jnp.float32)))
+        wide.append(times_mask(spread, to_lanes.astype(jnp.float32)))
     shading = sum(colour[c] * wide[c] for c in range(3))
-    after = exact_dot(weight * shading, beyond)
+    after = times_mask(weight * shading, beyond)
     ups[0] = (shading * leaving - after - wide[3]) * steps * logistic(raw)
     for c in range(3):
         ups[1 + c] = weight * wide[c] * colour[c] * (1.0 - colour[c])
@@ -263,25 +285,25 @@
         for ch in range(4):
             line = jnp.broadcast_to(ups[ch, pl.ds(g, 1), :], (8, LANES))
             up8 = jnp.where(row8 == 4 + ch, line, up8)
-        up = jnp.concatenate([jnp.zeros((ROWS - 8, LANES), jnp.float32), up8], axis=0)
-        up = up.astype(jnp.bfloat16)
+        up16 = jnp.concatenate([jnp.zeros((8, LANES), jnp.float32), up8], axis=0)
+        up16 = up16.astype(jnp.bfloat16)
+        up = jnp.concatenate([jnp.zeros((ROWS - 16, LANES), jnp.bfloat16), up16], axis=0)
         grad_hidden = jnp.dot(weight_t[b], up, preferred_element_type=jnp.float32)
         grad_before = (grad_hidden * slope[g].astype(jnp.float32)).astype(jnp.bfloat16)
         dims = (((1,), (1,)), ((), ()))
-        return lax.dot_general(
-            grad_before, encoded[g], dims, preferred_element_type=jnp.float32
-        ) + lax.dot_general(hidden[g], up, dims, preferred_element_type=jnp.float32)
+        first = lax.dot_general(
+            encoded[g], grad_before, dims, preferred_element_type=jnp.float32
+        )
+        last = lax.dot_general(up16, hidden[g], dims, preferred_element_type=jnp.float32)
+        return first[: ROWS - 16], first[ROWS - 16 :] + last
 
     @pl.loop(0, turns)
     def _(turn):
         terms = [backward(together * turn + i) for i in range(together)]
         for i in range(together):
-            grads_t[brick_list[0, together * turn + i]] += terms[i]
-
-    @pl.loop(0, bricks // few)
-    def _(turn):
-        for i in range(few):
-            grads[few * turn + i] = grads_t[few * turn + i].T
+            b = brick_list[0, together * turn + i]
+            grads[b, : ROWS - 16, :] += terms[i][0]
+            grads[b, ROWS - 16 :, :] += terms[i][1]
 
 
 def own_rays(gathered, encoded, steps, group_row, group_col, place_col, brick_of, target):
@@ -297,16 +319,22 @@
             jax.ShapeDtypeStruct((3, ray_rows), jnp.float32),
             jax.ShapeDtypeStruct((bricks, ROWS, HID), jnp.float32),
         ),
-        in_specs=[pl.BlockSpec(memory_space=pltpu.SMEM)] + [vmem] * 7,
+        in_specs=[
+            pl.BlockSpec(memory_space=pltpu.SMEM),
+            vmem,
+            pl.BlockSpec(memory_space=pl.ANY),
+        ]
+        + [vmem] * 5,
         out_specs=(vmem, vmem),
         scratch_shapes=[
             pltpu.VMEM((bricks, HID, ROWS), jnp.bfloat16),
-            pltpu.VMEM((bricks, HID, ROWS), jnp.float32),
             pltpu.VMEM((groups, HID, LANES), jnp.bfloat16),
             pltpu.VMEM((groups, HID, LANES), jnp.bfloat16),
             pltpu.VMEM((4, groups, LANES), jnp.float32),
             pltpu.VMEM((4, groups, LANES), jnp.float32),
             pltpu.VMEM((entries, 128), jnp.float32),
+            pltpu.VMEM(encoded.shape, encoded.dtype),
+            pltpu.SemaphoreType.DMA(()),
         ],
         compiler_params=pltpu.CompilerParams(vmem_limit_bytes=VMEM_BYTES),
         cost_estimate=pl.CostEstimate(

time: 115 us -> 108 us (0.939)
  Pallas kernels: 111 us -> 105 us
    pallas_call x1, Pallas kernels: 54.7 us -> 47.1 us  [own_rays(): pl.pallas_call(functools.partial(rays_kernel, groups, bricks, ray_rows),...]
    pallas_call x1, Pallas kernels: 30.9 us -> 32.5 us  [sum_and_scale(): pl.pallas_call(functools.partial(update_kernel, sizes), out_shape=(jax.Sh...]
where the time goes in v3:
time: 108 us
  Pallas kernels  105 us (97%)
  local copies, waits for them, and re-layouts  2.8 us (3%)
    pallas_call x1, Pallas kernels, own_rays(): pl.pallas_call(functools.partial(rays_kernel, groups, bricks, ray_rows),...  47.1 us
    pallas_call x1, Pallas kernels, sum_and_scale(): pl.pallas_call(functools.partial(update_kernel, sizes), out_shape=(jax.Sh...  32.5 us
    pallas_call x1, Pallas kernels, gather_weights(): pl.pallas_call(functools.partial(gather_kernel, sizes, groups), out_shape...  25.2 us
    unnamed x2, local copies, waits for them, and re-layouts  2.8 us

profile of v3, /device:TPU:1, one launch (start us, length us, event | category | flops | bytes accessed | tf_op | source)
XLA Modules:
  0.0 108.1 jit_solution(8950030720059375550)
XLA Ops:
  0.6 25.2 %gather_weights.1 = (f32[4,4,2,64,256]{4,3,2,1,0:T(8,128)}, bf16[120,64,256]{2,1,0:T(8,128)(2,1)}, f32[120,256]{1,0:T(8,128)}, s32[1,384]{1,0:T(1,128)}, s32[384...) custom-call(bf16[60,256]{1,0:T(8,128)(2,1)} %bitcast.14, bf16[4,256]{1,0:T(4,128)(2,1)} %bitcast.18, ...), custom_call_target="tpu_custom_call" | custom-call | tf_op jit(solution)/shard_map/gather_weights/pallas_call | solution.py:461
  25.8 47.1 %own_rays.1 = (f32[3,48]{1,0:T(4,128)}, f32[32,64,256]{2,1,0:T(8,128)}) custom-call(s32[1,128]{1,0:T(1,128)} %get-tuple-element.14.brick_list, f32[32,64,256]{2,1,0:T(8,128)} %bitcast.19, bf16[120,64,256]{2,1,0:T(8,128)(2,1)} %get-tuple-element.16.encoded_in, f32[120,256]{1,0:T(8,128)} %get-tuple-element.17.steps_in, s32[1,384]{1,0:T(1,128)} %get-tuple-element.18.group_row, ...), custom_call_target="tpu_custom_call" | custom-call | flops 5033164800 | bytes 4194304 | tf_op jit(solution)/shard_map/own_rays/pallas_call | solution.py:316
  72.9 32.5 %sum_and_scale.1 = (f32[60,256]{1,0:T(8,128)}, f32[4,256]{1,0:T(4,128)}) custom-call(f32[4,4,2,64,256]{4,3,2,1,0:T(8,128)} %bitcast.12), custom_call_target="tpu_custom_call" | custom-call | tf_op jit(solution)/shard_map/sum_and_scale/pallas_call | solution.py:580
  105.3 1.5 %copy.9 = f32[1,256,60]{1,0,2:T(1,128)} copy(f32[1,256,60]{1,2,0:T(8,128)} %bitcast.13) | data formatting | bytes 122880
  106.9 1.3 %copy.11 = f32[1,4,256]{2,1,0:T(4,128)} copy(f32[1,4,256]{2,1,0:T(4,128)} %bitcast.17) | data formatting | bytes 8192

commit v4 on v3

--- a/solution.py
+++ b/solution.py
@@ -182,7 +182,7 @@
     fetch = pltpu.make_async_copy(encoded_in, encoded, arrived)
     fetch.start()
     entries = ray_rows * SEGS
-    together = 8
+    together = 4
     turns = (brick_list[0, brick_list.shape[1] - 1] + together - 1) // together
     place = (iota((groups, entries), 0) == group_row[...]).astype(jnp.float32)
     outs[...] = jnp.zeros_like(outs)
@@ -295,15 +295,13 @@
             encoded[g], grad_before, dims, preferred_element_type=jnp.float32
         )
         last = lax.dot_general(up16, hidden[g], dims, preferred_element_type=jnp.float32)
-        return first[: ROWS - 16], first[ROWS - 16 :] + last
+        grads[b, : ROWS - 16, :] += first[: ROWS - 16]
+        grads[b, ROWS - 16 :, :] += first[ROWS - 16 :] + last
 
     @pl.loop(0, turns)
     def _(turn):
-        terms = [backward(together * turn + i) for i in range(together)]
         for i in range(together):
-            b = brick_list[0, together * turn + i]
-            grads[b, : ROWS - 16, :] += terms[i][0]
-            grads[b, ROWS - 16 :, :] += terms[i][1]
+            backward(together * turn + i)
 
 
 def own_rays(gathered, encoded, steps, group_row, group_col, place_col, brick_of, target):

time: 108 us -> 111 us (1.028); the launches traced: 108 us -> 110 us
  Pallas kernels: 105 us -> 107 us
    pallas_call x1, Pallas kernels: 47.1 us -> 52 us  [own_rays(): pl.pallas_call(functools.partial(rays_kernel, groups, bricks, ray_rows),...]
    pallas_call x1, Pallas kernels: 32.5 us -> 29.3 us  [sum_and_scale(): pl.pallas_call(functools.partial(update_kernel, sizes), out_shape=(jax.Sh...]
where the time goes in v4:
time: 111 us; the launch traced here: 110 us
  Pallas kernels  107 us (96%)
  local copies, waits for them, and re-layouts  2.8 us (3%)
    pallas_call x1, Pallas kernels, own_rays(): pl.pallas_call(functools.partial(rays_kernel, groups, bricks, ray_rows),...  52 us
    pallas_call x1, Pallas kernels, sum_and_scale(): pl.pallas_call(functools.partial(update_kernel, sizes), out_shape=(jax.Sh...  29.3 us
    pallas_call x1, Pallas kernels, gather_weights(): pl.pallas_call(functools.partial(gather_kernel, sizes, groups), out_shape...  25.2 us
    unnamed x2, local copies, waits for them, and re-layouts  2.8 us

profile of v4, /device:TPU:1, one launch (start us, length us, event | category | flops | bytes accessed | tf_op | source)
XLA Modules:
  0.0 110.0 jit_solution(10620043221566861853)
XLA Ops:
  0.6 25.2 %gather_weights.1 = (f32[4,4,2,64,256]{4,3,2,1,0:T(8,128)}, bf16[120,64,256]{2,1,0:T(8,128)(2,1)}, f32[120,256]{1,0:T(8,128)}, s32[1,384]{1,0:T(1,128)}, s32[384...) custom-call(bf16[60,256]{1,0:T(8,128)(2,1)} %bitcast.14, bf16[4,256]{1,0:T(4,128)(2,1)} %bitcast.18, ...), custom_call_target="tpu_custom_call" | custom-call | tf_op jit(solution)/shard_map/gather_weights/pallas_call | solution.py:459
  25.8 52.0 %own_rays.1 = (f32[3,48]{1,0:T(4,128)}, f32[32,64,256]{2,1,0:T(8,128)}) custom-call(s32[1,128]{1,0:T(1,128)} %get-tuple-element.14.brick_list, f32[32,64,256]{2,1,0:T(8,128)} %bitcast.19, bf16[120,64,256]{2,1,0:T(8,128)(2,1)} %get-tuple-element.16.encoded_in, f32[120,256]{1,0:T(8,128)} %get-tuple-element.17.steps_in, s32[1,384]{1,0:T(1,128)} %get-tuple-element.18.group_row, ...), custom_call_target="tpu_custom_call" | custom-call | flops 5033164800 | bytes 4194304 | tf_op jit(solution)/shard_map/own_rays/pallas_call | solution.py:314
  77.8 29.3 %sum_and_scale.1 = (f32[60,256]{1,0:T(8,128)}, f32[4,256]{1,0:T(4,128)}) custom-call(f32[4,4,2,64,256]{4,3,2,1,0:T(8,128)} %bitcast.12), custom_call_target="tpu_custom_call" | custom-call | tf_op jit(solution)/shard_map/sum_and_scale/pallas_call | solution.py:578
  107.2 1.5 %copy.9 = f32[1,256,60]{1,0,2:T(1,128)} copy(f32[1,256,60]{1,2,0:T(8,128)} %bitcast.13) | data formatting | bytes 122880
  108.7 1.3 %copy.11 = f32[1,4,256]{2,1,0:T(4,128)} copy(f32[1,4,256]{2,1,0:T(4,128)} %bitcast.17) | data formatting | bytes 8192
